TPU v7x, 512 devices: a whole 4x8x8 slice. The times are simulated.
512 devices in a mesh: pot: 128 (over z_lo, y, x, core), grid: 4 (over z_hi).
Axes of the slice: x: 4, y: 8, z: 8 (z_hi: 4, z_lo: 2; z = z_hi * 2 + z_lo), core: 2. Of those that a mesh axis runs over, the one named last changes fastest.
Arguments:
- potentials: float32 [128, 32, 4096], P('pot', 'grid'), may hold values from -24 to 24
- orbitals: bfloat16 [32, 32, 4096], P(None, 'grid', 'pot'), may hold values from -0.5 to 2
- energies: float32 [32], replicated, may hold values from -2 to -0.2
- local_potential: float32 [32, 4096], replicated, may hold values from 0 to 3
- inverse_factor: bfloat16 [128, 128], replicated, may hold values from -8 to 8, as said below
Outputs:
- updated: float32 [128, 32, 4096], P('pot', 'grid')
- margins: float32 [128, 128], P('pot')
Inputs may be any that keep to these rules, and one draw needn't show every extreme that they name: `inverse_factor`: lower triangular with a positive diagonal.
All inputs are finite; a program needn't handle non-finite values.
Results may differ from a plain program's by a relative error of at most 0.0029.
Values may be sent and summed in bfloat16 or wider, within the bound.
A program may use at most 64 MiB of HBM per device.

v0:
```python
import jax
import jax.numpy as jnp
from jax import lax
from jax.sharding import PartitionSpec as P

NX = 64
NY = 64
NZ = 32
ORBITALS = 32
BLOCKS = 4
SWEEPS = 4
DAMPING = 0.8


def padded_2(block, sides, width):
    for axis, dim in sides:
        count = lax.axis_size(axis)
        forward = [(i, i + 1) for i in range(count - 1)]
        backward = [(target, source) for source, target in forward]
        low = lax.ppermute(
            lax.slice_in_dim(block, block.shape[dim] - width, None, axis=dim), axis, forward
        )
        high = lax.ppermute(lax.slice_in_dim(block, 0, width, axis=dim), axis, backward)
        block = jnp.concatenate([low, block, high], axis=dim)
    return block


def plane_neighbours(field, row_width):
    plane_size = field.shape[-1]
    widths = [(0, 0)] * (field.ndim - 1)
    padded = jnp.pad(field, widths + [(row_width, row_width)])
    along_y = padded[..., 2 * row_width :] + padded[..., :plane_size]
    column = jnp.arange(plane_size, dtype=jnp.int32) % row_width
    padded = jnp.pad(field, widths + [(1, 1)])
    right_side = jnp.where(column == row_width - 1, 0.0, padded[..., 2:])
    left_side = jnp.where(column == 0, 0.0, padded[..., :plane_size])
    return along_y + right_side + left_side


def across_slabs(answer):
    padded = padded_2(answer, (("grid", 2),), 1)
    return padded[:, :, 2:] + padded[:, :, :-2]


def absorb(orbital_block, energy_block, fields, local_here, along_planes):
    orbital = orbital_block.astype(jnp.float32)[:, None]
    diagonal = (3.0 + local_here[None] - energy_block[:, None, None])[:, None]
    source = -orbital * fields[None]
    answer = DAMPING * source / diagonal
    for sweep_index in range(SWEEPS - 1):
        nearby = along_planes(answer) + plane_neighbours(answer, NX)
        answer = answer + DAMPING * (source - diagonal * answer + 0.5 * nearby) / diagonal
    return jnp.sum(orbital * answer, axis=0)


def local(potentials, orbitals, energies, local_potential, inverse_factor):
    slab_depth = potentials.shape[1]
    grid_index = lax.axis_index("grid")
    local_here = lax.dynamic_slice_in_dim(local_potential, grid_index * slab_depth, slab_depth, 0)
    block_size = ORBITALS // BLOCKS
    response = jnp.zeros(potentials.shape, jnp.float32)
    for number in range(BLOCKS):
        orbital_block = orbitals[number * block_size : (number + 1) * block_size]
        gathered = lax.all_gather(orbital_block, "pot", axis=2, tiled=True)
        energy_block = energies[number * block_size : (number + 1) * block_size]
        response = response + absorb(gathered, energy_block, potentials, local_here, across_slabs)
    trial_block = (potentials + 4.0 / ORBITALS * response).astype(jnp.bfloat16)
    by_cells = lax.all_to_all(trial_block, "pot", split_axis=2, concat_axis=0, tiled=True)
    row_count = by_cells.shape[0]
    flattened = by_cells.reshape(row_count, -1)
    partial_margins = lax.dot_general(
        flattened, flattened, (((1,), (1,)), ((), ())), preferred_element_type=jnp.float32
    )
    combined = jnp.dot(inverse_factor, flattened, preferred_element_type=jnp.float32).reshape(
        by_cells.shape
    )
    updated = lax.all_to_all(combined, "pot", split_axis=0, concat_axis=2, tiled=True)
    own_count = potentials.shape[0]
    summed_all = lax.psum(partial_margins, ("pot", "grid"))
    own_rows = lax.dynamic_slice_in_dim(summed_all, lax.axis_index("pot") * own_count, own_count, 0)
    margins = own_rows / (NX * NY * NZ)
    return (updated, margins)


def solution(mesh):
    in_specs = (P("pot", "grid", None), P(None, "grid", "pot"), P(), P(), P())
    out_specs = (P("pot", "grid", None), P("pot", None))
    return jax.shard_map(local, mesh=mesh, in_specs=in_specs, out_specs=out_specs, check_vma=False)
```

profile of v0, /device:TPU:1, one launch (start us, length us, event | category | flops | bytes accessed | tf_op | source)
XLA Modules:
  0.0 1255.0 jit_solution(13859245160564547657)
XLA Ops:
  8.1 192.4 %all_gather.12 = bf16[8,8,4096]{1,0,2:T(8,128)(2,1)} all-gather(bf16[8,8,32]{1,0,2:T(8,128)(2,1)S(1)} %copy.397), channel_id=1, replica_groups=mesh['pot'=128,'grid'=4] {'pot'}, dimensions={2}, use_global_device_ids=true | all-gather | bytes 528384 | tf_op jit(solution)/shard_map/all_gather | solution.py:64
  200.4 7.9 copy.321
  208.4 184.1 %all_gather.13 = bf16[8,8,4096]{1,0,2:T(8,128)(2,1)} all-gather(bf16[8,8,32]{1,0,2:T(8,128)(2,1)S(1)} %copy.398), channel_id=1, replica_groups=mesh['pot'=128,'grid'=4] {'pot'}, dimensions={2}, use_global_device_ids=true | all-gather | bytes 528384 | tf_op jit(solution)/shard_map/all_gather | solution.py:64
  392.5 7.9 copy.338
  400.5 185.2 %all_gather.14 = bf16[8,8,4096]{1,0,2:T(8,128)(2,1)} all-gather(bf16[8,8,32]{1,0,2:T(8,128)(2,1)S(1)} %copy.399), channel_id=1, replica_groups=mesh['pot'=128,'grid'=4] {'pot'}, dimensions={2}, use_global_device_ids=true | all-gather | bytes 528384 | tf_op jit(solution)/shard_map/all_gather | solution.py:64
  585.7 7.9 copy.355
  593.7 184.1 %all_gather.15 = bf16[8,8,4096]{1,0,2:T(8,128)(2,1)} all-gather(bf16[8,8,32]{1,0,2:T(8,128)(2,1)S(1)} %copy.400), channel_id=1, replica_groups=mesh['pot'=128,'grid'=4] {'pot'}, dimensions={2}, use_global_device_ids=true | all-gather | bytes 528384 | tf_op jit(solution)/shard_map/all_gather | solution.py:64
  777.8 7.9 copy.372
  789.7 6.4 collective-permute-start.7
  797.6 6.7 collective-permute-start.1
  806.6 6.1 collective-permute-start.13
  816.3 6.1 collective-permute-start.19
  825.8 6.1 collective-permute-start.9
  835.3 6.1 collective-permute-start.3
  844.9 6.1 collective-permute-start.15
  852.6 1.6 fusion.67
  854.5 6.1 collective-permute-start.21
  860.8 11.6 collective-permute-start.10
  872.5 1.6 fusion.64
  874.5 6.1 collective-permute-start.11
  882.2 1.6 fusion.70
  884.2 6.1 collective-permute-start.5
  891.9 1.6 fusion.73
  894.0 6.1 collective-permute-start.17
  903.1 6.1 collective-permute-start.23
  914.6 3.0 copy.392
  918.1 22.4 %reduce.4 = bf16[4096,8]{1,0:T(8,128)(2,1)S(1)} reduce(bf16[4096,1,8]{2,1,0:T(2,128)(2,1)S(1)} %bitcast.279, bf16[]{:T(256)} %broadcast.208), dimensions={1}, to_apply=%bitcast.262.reduce_sub_computation | reduce | bytes 131074
  941.6 21.8 %all_to_all.33 = bf16[128,2,128]{2,1,0:T(2,128)(2,1)S(1)} all-to-all(bf16[128,2,128]{2,1,0:T(2,128)(2,1)S(1)} %reshape.105), channel_id=1, replica_groups=mesh['pot'=128,'grid'=4] {'pot'}, dimensions={0} | all-to-all | bytes 131072 | tf_op jit(solution)/shard_map/all_to_all | solution.py:68
  963.4 2.8 reshape.106
  966.1 1.9 copy.393
  969.7 5.8 all-to-all-start.1
  976.4 267.5 %all-reduce.26.cloned.1.call-done = f32[128,128]{1,0:T(8,128)} async-done(((f32[128,128]{1,0:T(8,128)}), f32[128,128]{1,0:T(8,128)}) %all-reduce.26.cloned.1.call-update) | async-done | bytes 65552 | tf_op jit(solution)/shard_map/psum | solution.py:79
  (134 shorter events, 44.8 us)
Async XLA Ops:
  7.2 961.2 %copy-start = (bf16[128,128]{1,0:T(8,128)(2,1)S(1)}, bf16[128,128]{1,0:T(8,128)(2,1)}, u32[]{:S(2)}) copy-start(bf16[128,128]{1,0:T(8,128)(2,1)} %param.9) | copy-start | bytes 98308
  777.8 7.9 copy-start.2
  777.8 8.9 copy-start.1
  788.3 18.2 %collective-permute-start.6 = (f32[8,1,1,4096]{3,0,2,1:T(8,128)S(1)}, f32[8,1,1,4096]{3,0,2,1:T(8,128)S(1)}, u32[]{:S(2)}, u32[]{:S(2)}) collective-permute-start(f32[8,1,1,4096]{3,0,2,1:T(8,128)S(1)} %copy.339), channel_id=1, source_target_pairs={{1,0},{2,1},{3,2},{5,4},{6,5},{7,6},{9,8},{10,9},{11,10},{13,12},{... | collective-permute-start | bytes 393224 | tf_op jit(solution)/shard_map/ppermute | solution.py:23
  789.7 23.1 %collective-permute-start.7 = (f32[8,1,1,4096]{3,0,2,1:T(8,128)S(1)}, f32[8,1,1,4096]{3,0,2,1:T(8,128)S(1)}, u32[]{:S(2)}, u32[]{:S(2)}) collective-permute-start(f32[8,1,1,4096]{3,0,2,1:T(8,128)S(1)} %copy.341), channel_id=1, source_target_pairs={{0,1},{1,2},{2,3},{4,5},{5,6},{6,7},{8,9},{9,10},{10,11},{12,13},{... | collective-permute-start | bytes 393224 | tf_op jit(solution)/shard_map/ppermute | solution.py:20
  796.3 20.0 %collective-permute-start = (f32[8,1,1,4096]{3,0,2,1:T(8,128)S(1)}, f32[8,1,1,4096]{3,0,2,1:T(8,128)S(1)}, u32[]{:S(2)}, u32[]{:S(2)}) collective-permute-start(f32[8,1,1,4096]{3,0,2,1:T(8,128)S(1)} %copy.322), channel_id=1, source_target_pairs={{1,0},{2,1},{3,2},{5,4},{6,5},{7,6},{9,8},{10,9},{11,10},{13,12},{... | collective-permute-start | bytes 393224 | tf_op jit(solution)/shard_map/ppermute | solution.py:23
  797.6 24.9 %collective-permute-start.1 = (f32[8,1,1,4096]{3,0,2,1:T(8,128)S(1)}, f32[8,1,1,4096]{3,0,2,1:T(8,128)S(1)}, u32[]{:S(2)}, u32[]{:S(2)}) collective-permute-start(f32[8,1,1,4096]{3,0,2,1:T(8,128)S(1)} %copy.324), channel_id=1, source_target_pairs={{0,1},{1,2},{2,3},{4,5},{5,6},{6,7},{8,9},{9,10},{10,11},{12,13},{... | collective-permute-start | bytes 393224 | tf_op jit(solution)/shard_map/ppermute | solution.py:20
  805.0 20.8 %collective-permute-start.12 = (f32[8,1,1,4096]{3,0,2,1:T(8,128)S(1)}, f32[8,1,1,4096]{3,0,2,1:T(8,128)S(1)}, u32[]{:S(2)}, u32[]{:S(2)}) collective-permute-start(f32[8,1,1,4096]{3,0,2,1:T(8,128)S(1)} %copy.356), channel_id=1, source_target_pairs={{1,0},{2,1},{3,2},{5,4},{6,5},{7,6},{9,8},{10,9},{11,10},{13,12},{... | collective-permute-start | bytes 393224 | tf_op jit(solution)/shard_map/ppermute | solution.py:23
  806.6 25.4 %collective-permute-start.13 = (f32[8,1,1,4096]{3,0,2,1:T(8,128)S(1)}, f32[8,1,1,4096]{3,0,2,1:T(8,128)S(1)}, u32[]{:S(2)}, u32[]{:S(2)}) collective-permute-start(f32[8,1,1,4096]{3,0,2,1:T(8,128)S(1)} %copy.358), channel_id=1, source_target_pairs={{0,1},{1,2},{2,3},{4,5},{5,6},{6,7},{8,9},{9,10},{10,11},{12,13},{... | collective-permute-start | bytes 393224 | tf_op jit(solution)/shard_map/ppermute | solution.py:20
  812.8 22.4 %collective-permute-start.18 = (f32[8,1,1,4096]{3,0,2,1:T(8,128)S(1)}, f32[8,1,1,4096]{3,0,2,1:T(8,128)S(1)}, u32[]{:S(2)}, u32[]{:S(2)}) collective-permute-start(f32[8,1,1,4096]{3,0,2,1:T(8,128)S(1)} %copy.373), channel_id=1, source_target_pairs={{1,0},{2,1},{3,2},{5,4},{6,5},{7,6},{9,8},{10,9},{11,10},{13,12},{... | collective-permute-start | bytes 393224 | tf_op jit(solution)/shard_map/ppermute | solution.py:23
  816.3 25.3 %collective-permute-start.19 = (f32[8,1,1,4096]{3,0,2,1:T(8,128)S(1)}, f32[8,1,1,4096]{3,0,2,1:T(8,128)S(1)}, u32[]{:S(2)}, u32[]{:S(2)}) collective-permute-start(f32[8,1,1,4096]{3,0,2,1:T(8,128)S(1)} %copy.375), channel_id=1, source_target_pairs={{0,1},{1,2},{2,3},{4,5},{5,6},{6,7},{8,9},{9,10},{10,11},{12,13},{... | collective-permute-start | bytes 393224 | tf_op jit(solution)/shard_map/ppermute | solution.py:20
  822.5 22.3 %collective-permute-start.8 = (f32[8,1,1,4096]{3,0,2,1:T(8,128)S(1)}, f32[8,1,1,4096]{3,0,2,1:T(8,128)S(1)}, u32[]{:S(2)}, u32[]{:S(2)}) collective-permute-start(f32[8,1,1,4096]{3,0,2,1:T(8,128)S(1)} %copy.344), channel_id=1, source_target_pairs={{1,0},{2,1},{3,2},{5,4},{6,5},{7,6},{9,8},{10,9},{11,10},{13,12},{... | collective-permute-start | bytes 393224 | tf_op jit(solution)/shard_map/ppermute | solution.py:23
  825.8 25.4 %collective-permute-start.9 = (f32[8,1,1,4096]{3,0,2,1:T(8,128)S(1)}, f32[8,1,1,4096]{3,0,2,1:T(8,128)S(1)}, u32[]{:S(2)}, u32[]{:S(2)}) collective-permute-start(f32[8,1,1,4096]{3,0,2,1:T(8,128)S(1)} %copy.346), channel_id=1, source_target_pairs={{0,1},{1,2},{2,3},{4,5},{5,6},{6,7},{8,9},{9,10},{10,11},{12,13},{... | collective-permute-start | bytes 393224 | tf_op jit(solution)/shard_map/ppermute | solution.py:20
  832.0 22.5 %collective-permute-start.2 = (f32[8,1,1,4096]{3,0,2,1:T(8,128)S(1)}, f32[8,1,1,4096]{3,0,2,1:T(8,128)S(1)}, u32[]{:S(2)}, u32[]{:S(2)}) collective-permute-start(f32[8,1,1,4096]{3,0,2,1:T(8,128)S(1)} %copy.327), channel_id=1, source_target_pairs={{1,0},{2,1},{3,2},{5,4},{6,5},{7,6},{9,8},{10,9},{11,10},{13,12},{... | collective-permute-start | bytes 393224 | tf_op jit(solution)/shard_map/ppermute | solution.py:23
  835.3 25.5 %collective-permute-start.3 = (f32[8,1,1,4096]{3,0,2,1:T(8,128)S(1)}, f32[8,1,1,4096]{3,0,2,1:T(8,128)S(1)}, u32[]{:S(2)}, u32[]{:S(2)}) collective-permute-start(f32[8,1,1,4096]{3,0,2,1:T(8,128)S(1)} %copy.329), channel_id=1, source_target_pairs={{0,1},{1,2},{2,3},{4,5},{5,6},{6,7},{8,9},{9,10},{10,11},{12,13},{... | collective-permute-start | bytes 393224 | tf_op jit(solution)/shard_map/ppermute | solution.py:20
  841.5 32.9 %collective-permute-start.14 = (f32[8,1,1,4096]{3,0,2,1:T(8,128)S(1)}, f32[8,1,1,4096]{3,0,2,1:T(8,128)S(1)}, u32[]{:S(2)}, u32[]{:S(2)}) collective-permute-start(f32[8,1,1,4096]{3,0,2,1:T(8,128)S(1)} %copy.361), channel_id=1, source_target_pairs={{1,0},{2,1},{3,2},{5,4},{6,5},{7,6},{9,8},{10,9},{11,10},{13,12},{... | collective-permute-start | bytes 393224 | tf_op jit(solution)/shard_map/ppermute | solution.py:23
  844.9 35.9 %collective-permute-start.15 = (f32[8,1,1,4096]{3,0,2,1:T(8,128)S(1)}, f32[8,1,1,4096]{3,0,2,1:T(8,128)S(1)}, u32[]{:S(2)}, u32[]{:S(2)}) collective-permute-start(f32[8,1,1,4096]{3,0,2,1:T(8,128)S(1)} %copy.363), channel_id=1, source_target_pairs={{0,1},{1,2},{2,3},{4,5},{5,6},{6,7},{8,9},{9,10},{10,11},{12,13},{... | collective-permute-start | bytes 393224 | tf_op jit(solution)/shard_map/ppermute | solution.py:20
  851.1 33.0 %collective-permute-start.20 = (f32[8,1,1,4096]{3,0,2,1:T(8,128)S(1)}, f32[8,1,1,4096]{3,0,2,1:T(8,128)S(1)}, u32[]{:S(2)}, u32[]{:S(2)}) collective-permute-start(f32[8,1,1,4096]{3,0,2,1:T(8,128)S(1)} %copy.378), channel_id=1, source_target_pairs={{1,0},{2,1},{3,2},{5,4},{6,5},{7,6},{9,8},{10,9},{11,10},{13,12},{... | collective-permute-start | bytes 393224 | tf_op jit(solution)/shard_map/ppermute | solution.py:23
  854.5 35.9 %collective-permute-start.21 = (f32[8,1,1,4096]{3,0,2,1:T(8,128)S(1)}, f32[8,1,1,4096]{3,0,2,1:T(8,128)S(1)}, u32[]{:S(2)}, u32[]{:S(2)}) collective-permute-start(f32[8,1,1,4096]{3,0,2,1:T(8,128)S(1)} %copy.380), channel_id=1, source_target_pairs={{0,1},{1,2},{2,3},{4,5},{5,6},{6,7},{8,9},{9,10},{10,11},{12,13},{... | collective-permute-start | bytes 393224 | tf_op jit(solution)/shard_map/ppermute | solution.py:20
  860.8 33.2 %collective-permute-start.10 = (f32[8,1,1,4096]{3,0,2,1:T(8,128)S(1)}, f32[8,1,1,4096]{3,0,2,1:T(8,128)S(1)}, u32[]{:S(2)}, u32[]{:S(2)}) collective-permute-start(f32[8,1,1,4096]{3,0,2,1:T(8,128)S(1)} %copy.349), channel_id=1, source_target_pairs={{1,0},{2,1},{3,2},{5,4},{6,5},{7,6},{9,8},{10,9},{11,10},{13,12},{... | collective-permute-start | bytes 393224 | tf_op jit(solution)/shard_map/ppermute | solution.py:23
  874.5 25.7 %collective-permute-start.11 = (f32[8,1,1,4096]{3,0,2,1:T(8,128)S(1)}, f32[8,1,1,4096]{3,0,2,1:T(8,128)S(1)}, u32[]{:S(2)}, u32[]{:S(2)}) collective-permute-start(f32[8,1,1,4096]{3,0,2,1:T(8,128)S(1)} %copy.351), channel_id=1, source_target_pairs={{0,1},{1,2},{2,3},{4,5},{5,6},{6,7},{8,9},{9,10},{10,11},{12,13},{... | collective-permute-start | bytes 393224 | tf_op jit(solution)/shard_map/ppermute | solution.py:20
  880.7 22.4 %collective-permute-start.4 = (f32[8,1,1,4096]{3,0,2,1:T(8,128)S(1)}, f32[8,1,1,4096]{3,0,2,1:T(8,128)S(1)}, u32[]{:S(2)}, u32[]{:S(2)}) collective-permute-start(f32[8,1,1,4096]{3,0,2,1:T(8,128)S(1)} %copy.332), channel_id=1, source_target_pairs={{1,0},{2,1},{3,2},{5,4},{6,5},{7,6},{9,8},{10,9},{11,10},{13,12},{... | collective-permute-start | bytes 393224 | tf_op jit(solution)/shard_map/ppermute | solution.py:23
  884.2 25.2 %collective-permute-start.5 = (f32[8,1,1,4096]{3,0,2,1:T(8,128)S(1)}, f32[8,1,1,4096]{3,0,2,1:T(8,128)S(1)}, u32[]{:S(2)}, u32[]{:S(2)}) collective-permute-start(f32[8,1,1,4096]{3,0,2,1:T(8,128)S(1)} %copy.334), channel_id=1, source_target_pairs={{0,1},{1,2},{2,3},{4,5},{5,6},{6,7},{8,9},{9,10},{10,11},{12,13},{... | collective-permute-start | bytes 393224 | tf_op jit(solution)/shard_map/ppermute | solution.py:20
  890.4 20.6 %collective-permute-start.16 = (f32[8,1,1,4096]{3,0,2,1:T(8,128)S(1)}, f32[8,1,1,4096]{3,0,2,1:T(8,128)S(1)}, u32[]{:S(2)}, u32[]{:S(2)}) collective-permute-start(f32[8,1,1,4096]{3,0,2,1:T(8,128)S(1)} %copy.366), channel_id=1, source_target_pairs={{1,0},{2,1},{3,2},{5,4},{6,5},{7,6},{9,8},{10,9},{11,10},{13,12},{... | collective-permute-start | bytes 393224 | tf_op jit(solution)/shard_map/ppermute | solution.py:23
  894.0 17.2 %collective-permute-start.17 = (f32[8,1,1,4096]{3,0,2,1:T(8,128)S(1)}, f32[8,1,1,4096]{3,0,2,1:T(8,128)S(1)}, u32[]{:S(2)}, u32[]{:S(2)}) collective-permute-start(f32[8,1,1,4096]{3,0,2,1:T(8,128)S(1)} %copy.368), channel_id=1, source_target_pairs={{0,1},{1,2},{2,3},{4,5},{5,6},{6,7},{8,9},{9,10},{10,11},{12,13},{... | collective-permute-start | bytes 393224 | tf_op jit(solution)/shard_map/ppermute | solution.py:20
  900.2 12.6 %collective-permute-start.22 = (f32[8,1,1,4096]{3,0,2,1:T(8,128)S(1)}, f32[8,1,1,4096]{3,0,2,1:T(8,128)S(1)}, u32[]{:S(2)}, u32[]{:S(2)}) collective-permute-start(f32[8,1,1,4096]{3,0,2,1:T(8,128)S(1)} %copy.383), channel_id=1, source_target_pairs={{1,0},{2,1},{3,2},{5,4},{6,5},{7,6},{9,8},{10,9},{11,10},{13,12},{... | collective-permute-start | bytes 393224 | tf_op jit(solution)/shard_map/ppermute | solution.py:23
  903.1 9.8 collective-permute-start.23
  969.7 275.5 %all-to-all-start.1 = ((f32[128,1,256]{2,1,0:T(1,128)}), f32[128,1,256]{2,1,0:T(1,128)S(1)}, u32[]{:S(2)}, u32[]{:S(2)}) async-start(f32[128,1,256]{2,1,0:T(1,128)} %reshape.107), calls=%async_computation.1 | async-start | bytes 262144 | tf_op jit(solution)/shard_map/all_to_all | solution.py:77
  975.5 268.4 %all-reduce.26.cloned.1.call-start = ((), (), s32[]{:S(2)}) async-start(), calls=%async_computation.2 | async-start | bytes 131072 | tf_op jit(solution)/shard_map/psum | solution.py:79
Sparse Core Ops, SparseCore 0:
  981.3 262.5 all-reduce.25
where the time goes:
time: 1260 us; the launch traced here: 1250 us
  blocking collectives  768 us (61%)
  waiting for transfers between devices  268 us (21%)
  starting transfers between devices  106 us (8%)
  local copies, waits for them, and re-layouts  52.8 us (4%)
  other arithmetic  44.6 us (4%)
  between operations  15.4 us (1%)
    all_gather x4, blocking collectives, local(): gathered = lax.all_gather(orbital_block, 'pot', axis=2, tiled=True)  746 us
    psum x1, waiting for transfers between devices, local(): summed_all = lax.psum(partial_margins, ('pot', 'grid'))  268 us
    ppermute x12, starting transfers between devices, padded_2(): lax.ppermute(lax.slice_in_dim(block, block.shape[dim] - width, None, axis...  74.2 us
    all_gather x4, local copies, waits for them, and re-layouts, local(): gathered = lax.all_gather(orbital_block, 'pot', axis=2, tiled=True)  31.5 us
    ppermute x12, starting transfers between devices, padded_2(): lax.ppermute(lax.slice_in_dim(block, 0, width, axis=dim), axis, backward)  26 us
  transfers between devices with their start and end apart: 26, of which 1 were waited for; matrix products, arithmetic and copies ran while one was open for 2% of the time, Pallas kernels for 0%

commit v1 on v0

--- a/solution.py
+++ b/solution.py
@@ -76,7 +76,7 @@
     )
     updated = lax.all_to_all(combined, "pot", split_axis=0, concat_axis=2, tiled=True)
     own_count = potentials.shape[0]
-    summed_all = lax.psum(partial_margins, ("pot", "grid"))
+    summed_all = lax.psum(lax.psum(partial_margins, "pot"), "grid")
     own_rows = lax.dynamic_slice_in_dim(summed_all, lax.axis_index("pot") * own_count, own_count, 0)
     margins = own_rows / (NX * NY * NZ)
     return (updated, margins)

time: 1260 us -> 1990 us (1.58)
  waiting for transfers between devices: 268 us -> 989 us
    psum x1 -> x2, waiting for transfers between devices: 268 us -> 989 us  [local(): summed_all = lax.psum(lax.psum(partial_margins, 'pot'), 'grid')]
  transfers between devices with their start and end apart: 26 -> 27, of which waited for: 1 -> 2; matrix products, arithmetic and copies ran while one was open for 2% -> 1% of each run, Pallas kernels for 0% -> 0%
where the time goes in v1:
time: 1990 us; the launch traced here: 1980 us
  waiting for transfers between devices  989 us (50%)
  blocking collectives  768 us (39%)
  starting transfers between devices  106 us (5%)
  local copies, waits for them, and re-layouts  52.8 us (3%)
  other arithmetic  44.6 us (2%)
    psum x2, waiting for transfers between devices, local(): summed_all = lax.psum(lax.psum(partial_margins, 'pot'), 'grid')  989 us
    all_gather x4, blocking collectives, local(): gathered = lax.all_gather(orbital_block, 'pot', axis=2, tiled=True)  746 us
    ppermute x12, starting transfers between devices, padded_2(): lax.ppermute(lax.slice_in_dim(block, block.shape[dim] - width, None, axis...  74.2 us
  transfers between devices with their start and end apart: 27, of which 2 were waited for; matrix products, arithmetic and copies ran while one was open for 1% of the time, Pallas kernels for 0%

profile of v1, /device:TPU:1, one launch (start us, length us, event | category | flops | bytes accessed | tf_op | source)
XLA Modules:
  0.0 1976.2 jit_solution(16989125938899107293)
XLA Ops:
  8.1 192.4 %all_gather.12 = bf16[8,8,4096]{1,0,2:T(8,128)(2,1)} all-gather(bf16[8,8,32]{1,0,2:T(8,128)(2,1)S(1)} %copy.397), channel_id=1, replica_groups=mesh['pot'=128,'grid'=4] {'pot'}, dimensions={2}, use_global_device_ids=true | all-gather | bytes 528384 | tf_op jit(solution)/shard_map/all_gather | solution.py:64
  200.4 7.9 copy.321
  208.4 184.1 %all_gather.13 = bf16[8,8,4096]{1,0,2:T(8,128)(2,1)} all-gather(bf16[8,8,32]{1,0,2:T(8,128)(2,1)S(1)} %copy.398), channel_id=1, replica_groups=mesh['pot'=128,'grid'=4] {'pot'}, dimensions={2}, use_global_device_ids=true | all-gather | bytes 528384 | tf_op jit(solution)/shard_map/all_gather | solution.py:64
  392.5 7.9 copy.338
  400.5 185.2 %all_gather.14 = bf16[8,8,4096]{1,0,2:T(8,128)(2,1)} all-gather(bf16[8,8,32]{1,0,2:T(8,128)(2,1)S(1)} %copy.399), channel_id=1, replica_groups=mesh['pot'=128,'grid'=4] {'pot'}, dimensions={2}, use_global_device_ids=true | all-gather | bytes 528384 | tf_op jit(solution)/shard_map/all_gather | solution.py:64
  585.7 7.9 copy.355
  593.7 184.1 %all_gather.15 = bf16[8,8,4096]{1,0,2:T(8,128)(2,1)} all-gather(bf16[8,8,32]{1,0,2:T(8,128)(2,1)S(1)} %copy.400), channel_id=1, replica_groups=mesh['pot'=128,'grid'=4] {'pot'}, dimensions={2}, use_global_device_ids=true | all-gather | bytes 528384 | tf_op jit(solution)/shard_map/all_gather | solution.py:64
  777.8 7.9 copy.372
  789.7 6.4 collective-permute-start.7
  797.6 6.7 collective-permute-start.1
  806.6 6.1 collective-permute-start.13
  816.3 6.1 collective-permute-start.19
  825.8 6.1 collective-permute-start.9
  835.3 6.1 collective-permute-start.3
  844.9 6.1 collective-permute-start.15
  854.5 6.1 collective-permute-start.21
  860.8 11.6 collective-permute-start.10
  872.5 1.6 fusion.64
  874.5 6.1 collective-permute-start.11
  882.2 1.6 fusion.70
  884.2 6.1 collective-permute-start.5
  891.9 1.6 fusion.73
  894.0 6.1 collective-permute-start.17
  903.1 6.1 collective-permute-start.23
  914.6 3.0 copy.392
  918.1 22.4 %reduce.4 = bf16[4096,8]{1,0:T(8,128)(2,1)S(1)} reduce(bf16[4096,1,8]{2,1,0:T(2,128)(2,1)S(1)} %bitcast.279, bf16[]{:T(256)} %broadcast.208), dimensions={1}, to_apply=%bitcast.262.reduce_sub_computation | reduce | bytes 131074
  941.6 21.8 %all_to_all.33 = bf16[128,2,128]{2,1,0:T(2,128)(2,1)S(1)} all-to-all(bf16[128,2,128]{2,1,0:T(2,128)(2,1)S(1)} %reshape.105), channel_id=1, replica_groups=mesh['pot'=128,'grid'=4] {'pot'}, dimensions={0} | all-to-all | bytes 131072 | tf_op jit(solution)/shard_map/all_to_all | solution.py:68
  963.4 2.8 reshape.106
  966.1 1.9 copy.393
  969.7 5.8 all-to-all-start.1
  976.5 935.9 %all-reduce.27.cloned.1.call-done = f32[128,128]{1,0:T(8,128)} async-done(((f32[128,128]{1,0:T(8,128)}), f32[128,128]{1,0:T(8,128)}) %all-reduce.27.cloned.1.call-update) | async-done | bytes 65552 | tf_op jit(solution)/shard_map/psum | solution.py:79
  1912.4 52.8 %all-reduce.29.cloned.1.call-done = f32[128,128]{1,0:T(8,128)} async-done(((f32[128,128]{1,0:T(8,128)}), f32[128,128]{1,0:T(8,128)}) %all-reduce.29.cloned.1.call-update) | async-done | bytes 65552 | tf_op jit(solution)/shard_map/psum | solution.py:79
  (137 shorter events, 46.5 us)
Async XLA Ops:
  7.2 961.2 %copy-start = (bf16[128,128]{1,0:T(8,128)(2,1)S(1)}, bf16[128,128]{1,0:T(8,128)(2,1)}, u32[]{:S(2)}) copy-start(bf16[128,128]{1,0:T(8,128)(2,1)} %param.9) | copy-start | bytes 98308
  777.8 7.9 copy-start.2
  777.8 8.9 copy-start.1
  788.3 18.2 collective-permute-start.6
  789.7 23.1 %collective-permute-start.7 = (f32[8,1,1,4096]{3,0,2,1:T(8,128)S(1)}, f32[8,1,1,4096]{3,0,2,1:T(8,128)S(1)}, u32[]{:S(2)}, u32[]{:S(2)}) collective-permute-start(f32[8,1,1,4096]{3,0,2,1:T(8,128)S(1)} %copy.341), channel_id=1, source_target_pairs={{0,1},{1,2},{2,3},{4,5},{5,6},{6,7},{8,9},{9,10},{10,11},{12,13},{... | collective-permute-start | bytes 393224 | tf_op jit(solution)/shard_map/ppermute | solution.py:20
  796.3 20.0 %collective-permute-start = (f32[8,1,1,4096]{3,0,2,1:T(8,128)S(1)}, f32[8,1,1,4096]{3,0,2,1:T(8,128)S(1)}, u32[]{:S(2)}, u32[]{:S(2)}) collective-permute-start(f32[8,1,1,4096]{3,0,2,1:T(8,128)S(1)} %copy.322), channel_id=1, source_target_pairs={{1,0},{2,1},{3,2},{5,4},{6,5},{7,6},{9,8},{10,9},{11,10},{13,12},{... | collective-permute-start | bytes 393224 | tf_op jit(solution)/shard_map/ppermute | solution.py:23
  797.6 24.9 %collective-permute-start.1 = (f32[8,1,1,4096]{3,0,2,1:T(8,128)S(1)}, f32[8,1,1,4096]{3,0,2,1:T(8,128)S(1)}, u32[]{:S(2)}, u32[]{:S(2)}) collective-permute-start(f32[8,1,1,4096]{3,0,2,1:T(8,128)S(1)} %copy.324), channel_id=1, source_target_pairs={{0,1},{1,2},{2,3},{4,5},{5,6},{6,7},{8,9},{9,10},{10,11},{12,13},{... | collective-permute-start | bytes 393224 | tf_op jit(solution)/shard_map/ppermute | solution.py:20
  805.0 20.8 %collective-permute-start.12 = (f32[8,1,1,4096]{3,0,2,1:T(8,128)S(1)}, f32[8,1,1,4096]{3,0,2,1:T(8,128)S(1)}, u32[]{:S(2)}, u32[]{:S(2)}) collective-permute-start(f32[8,1,1,4096]{3,0,2,1:T(8,128)S(1)} %copy.356), channel_id=1, source_target_pairs={{1,0},{2,1},{3,2},{5,4},{6,5},{7,6},{9,8},{10,9},{11,10},{13,12},{... | collective-permute-start | bytes 393224 | tf_op jit(solution)/shard_map/ppermute | solution.py:23
  806.6 25.4 %collective-permute-start.13 = (f32[8,1,1,4096]{3,0,2,1:T(8,128)S(1)}, f32[8,1,1,4096]{3,0,2,1:T(8,128)S(1)}, u32[]{:S(2)}, u32[]{:S(2)}) collective-permute-start(f32[8,1,1,4096]{3,0,2,1:T(8,128)S(1)} %copy.358), channel_id=1, source_target_pairs={{0,1},{1,2},{2,3},{4,5},{5,6},{6,7},{8,9},{9,10},{10,11},{12,13},{... | collective-permute-start | bytes 393224 | tf_op jit(solution)/shard_map/ppermute | solution.py:20
  812.8 22.4 %collective-permute-start.18 = (f32[8,1,1,4096]{3,0,2,1:T(8,128)S(1)}, f32[8,1,1,4096]{3,0,2,1:T(8,128)S(1)}, u32[]{:S(2)}, u32[]{:S(2)}) collective-permute-start(f32[8,1,1,4096]{3,0,2,1:T(8,128)S(1)} %copy.373), channel_id=1, source_target_pairs={{1,0},{2,1},{3,2},{5,4},{6,5},{7,6},{9,8},{10,9},{11,10},{13,12},{... | collective-permute-start | bytes 393224 | tf_op jit(solution)/shard_map/ppermute | solution.py:23
  816.3 25.3 %collective-permute-start.19 = (f32[8,1,1,4096]{3,0,2,1:T(8,128)S(1)}, f32[8,1,1,4096]{3,0,2,1:T(8,128)S(1)}, u32[]{:S(2)}, u32[]{:S(2)}) collective-permute-start(f32[8,1,1,4096]{3,0,2,1:T(8,128)S(1)} %copy.375), channel_id=1, source_target_pairs={{0,1},{1,2},{2,3},{4,5},{5,6},{6,7},{8,9},{9,10},{10,11},{12,13},{... | collective-permute-start | bytes 393224 | tf_op jit(solution)/shard_map/ppermute | solution.py:20
  822.5 22.3 %collective-permute-start.8 = (f32[8,1,1,4096]{3,0,2,1:T(8,128)S(1)}, f32[8,1,1,4096]{3,0,2,1:T(8,128)S(1)}, u32[]{:S(2)}, u32[]{:S(2)}) collective-permute-start(f32[8,1,1,4096]{3,0,2,1:T(8,128)S(1)} %copy.344), channel_id=1, source_target_pairs={{1,0},{2,1},{3,2},{5,4},{6,5},{7,6},{9,8},{10,9},{11,10},{13,12},{... | collective-permute-start | bytes 393224 | tf_op jit(solution)/shard_map/ppermute | solution.py:23
  825.8 25.4 %collective-permute-start.9 = (f32[8,1,1,4096]{3,0,2,1:T(8,128)S(1)}, f32[8,1,1,4096]{3,0,2,1:T(8,128)S(1)}, u32[]{:S(2)}, u32[]{:S(2)}) collective-permute-start(f32[8,1,1,4096]{3,0,2,1:T(8,128)S(1)} %copy.346), channel_id=1, source_target_pairs={{0,1},{1,2},{2,3},{4,5},{5,6},{6,7},{8,9},{9,10},{10,11},{12,13},{... | collective-permute-start | bytes 393224 | tf_op jit(solution)/shard_map/ppermute | solution.py:20
  832.0 22.5 %collective-permute-start.2 = (f32[8,1,1,4096]{3,0,2,1:T(8,128)S(1)}, f32[8,1,1,4096]{3,0,2,1:T(8,128)S(1)}, u32[]{:S(2)}, u32[]{:S(2)}) collective-permute-start(f32[8,1,1,4096]{3,0,2,1:T(8,128)S(1)} %copy.327), channel_id=1, source_target_pairs={{1,0},{2,1},{3,2},{5,4},{6,5},{7,6},{9,8},{10,9},{11,10},{13,12},{... | collective-permute-start | bytes 393224 | tf_op jit(solution)/shard_map/ppermute | solution.py:23
  835.3 25.5 %collective-permute-start.3 = (f32[8,1,1,4096]{3,0,2,1:T(8,128)S(1)}, f32[8,1,1,4096]{3,0,2,1:T(8,128)S(1)}, u32[]{:S(2)}, u32[]{:S(2)}) collective-permute-start(f32[8,1,1,4096]{3,0,2,1:T(8,128)S(1)} %copy.329), channel_id=1, source_target_pairs={{0,1},{1,2},{2,3},{4,5},{5,6},{6,7},{8,9},{9,10},{10,11},{12,13},{... | collective-permute-start | bytes 393224 | tf_op jit(solution)/shard_map/ppermute | solution.py:20
  841.5 32.9 %collective-permute-start.14 = (f32[8,1,1,4096]{3,0,2,1:T(8,128)S(1)}, f32[8,1,1,4096]{3,0,2,1:T(8,128)S(1)}, u32[]{:S(2)}, u32[]{:S(2)}) collective-permute-start(f32[8,1,1,4096]{3,0,2,1:T(8,128)S(1)} %copy.361), channel_id=1, source_target_pairs={{1,0},{2,1},{3,2},{5,4},{6,5},{7,6},{9,8},{10,9},{11,10},{13,12},{... | collective-permute-start | bytes 393224 | tf_op jit(solution)/shard_map/ppermute | solution.py:23
  844.9 35.9 %collective-permute-start.15 = (f32[8,1,1,4096]{3,0,2,1:T(8,128)S(1)}, f32[8,1,1,4096]{3,0,2,1:T(8,128)S(1)}, u32[]{:S(2)}, u32[]{:S(2)}) collective-permute-start(f32[8,1,1,4096]{3,0,2,1:T(8,128)S(1)} %copy.363), channel_id=1, source_target_pairs={{0,1},{1,2},{2,3},{4,5},{5,6},{6,7},{8,9},{9,10},{10,11},{12,13},{... | collective-permute-start | bytes 393224 | tf_op jit(solution)/shard_map/ppermute | solution.py:20
  851.1 33.0 %collective-permute-start.20 = (f32[8,1,1,4096]{3,0,2,1:T(8,128)S(1)}, f32[8,1,1,4096]{3,0,2,1:T(8,128)S(1)}, u32[]{:S(2)}, u32[]{:S(2)}) collective-permute-start(f32[8,1,1,4096]{3,0,2,1:T(8,128)S(1)} %copy.378), channel_id=1, source_target_pairs={{1,0},{2,1},{3,2},{5,4},{6,5},{7,6},{9,8},{10,9},{11,10},{13,12},{... | collective-permute-start | bytes 393224 | tf_op jit(solution)/shard_map/ppermute | solution.py:23
  854.5 35.9 %collective-permute-start.21 = (f32[8,1,1,4096]{3,0,2,1:T(8,128)S(1)}, f32[8,1,1,4096]{3,0,2,1:T(8,128)S(1)}, u32[]{:S(2)}, u32[]{:S(2)}) collective-permute-start(f32[8,1,1,4096]{3,0,2,1:T(8,128)S(1)} %copy.380), channel_id=1, source_target_pairs={{0,1},{1,2},{2,3},{4,5},{5,6},{6,7},{8,9},{9,10},{10,11},{12,13},{... | collective-permute-start | bytes 393224 | tf_op jit(solution)/shard_map/ppermute | solution.py:20
  860.8 33.2 %collective-permute-start.10 = (f32[8,1,1,4096]{3,0,2,1:T(8,128)S(1)}, f32[8,1,1,4096]{3,0,2,1:T(8,128)S(1)}, u32[]{:S(2)}, u32[]{:S(2)}) collective-permute-start(f32[8,1,1,4096]{3,0,2,1:T(8,128)S(1)} %copy.349), channel_id=1, source_target_pairs={{1,0},{2,1},{3,2},{5,4},{6,5},{7,6},{9,8},{10,9},{11,10},{13,12},{... | collective-permute-start | bytes 393224 | tf_op jit(solution)/shard_map/ppermute | solution.py:23
  874.5 25.7 %collective-permute-start.11 = (f32[8,1,1,4096]{3,0,2,1:T(8,128)S(1)}, f32[8,1,1,4096]{3,0,2,1:T(8,128)S(1)}, u32[]{:S(2)}, u32[]{:S(2)}) collective-permute-start(f32[8,1,1,4096]{3,0,2,1:T(8,128)S(1)} %copy.351), channel_id=1, source_target_pairs={{0,1},{1,2},{2,3},{4,5},{5,6},{6,7},{8,9},{9,10},{10,11},{12,13},{... | collective-permute-start | bytes 393224 | tf_op jit(solution)/shard_map/ppermute | solution.py:20
  880.7 22.4 %collective-permute-start.4 = (f32[8,1,1,4096]{3,0,2,1:T(8,128)S(1)}, f32[8,1,1,4096]{3,0,2,1:T(8,128)S(1)}, u32[]{:S(2)}, u32[]{:S(2)}) collective-permute-start(f32[8,1,1,4096]{3,0,2,1:T(8,128)S(1)} %copy.332), channel_id=1, source_target_pairs={{1,0},{2,1},{3,2},{5,4},{6,5},{7,6},{9,8},{10,9},{11,10},{13,12},{... | collective-permute-start | bytes 393224 | tf_op jit(solution)/shard_map/ppermute | solution.py:23
  884.2 25.2 %collective-permute-start.5 = (f32[8,1,1,4096]{3,0,2,1:T(8,128)S(1)}, f32[8,1,1,4096]{3,0,2,1:T(8,128)S(1)}, u32[]{:S(2)}, u32[]{:S(2)}) collective-permute-start(f32[8,1,1,4096]{3,0,2,1:T(8,128)S(1)} %copy.334), channel_id=1, source_target_pairs={{0,1},{1,2},{2,3},{4,5},{5,6},{6,7},{8,9},{9,10},{10,11},{12,13},{... | collective-permute-start | bytes 393224 | tf_op jit(solution)/shard_map/ppermute | solution.py:20
  890.4 20.6 %collective-permute-start.16 = (f32[8,1,1,4096]{3,0,2,1:T(8,128)S(1)}, f32[8,1,1,4096]{3,0,2,1:T(8,128)S(1)}, u32[]{:S(2)}, u32[]{:S(2)}) collective-permute-start(f32[8,1,1,4096]{3,0,2,1:T(8,128)S(1)} %copy.366), channel_id=1, source_target_pairs={{1,0},{2,1},{3,2},{5,4},{6,5},{7,6},{9,8},{10,9},{11,10},{13,12},{... | collective-permute-start | bytes 393224 | tf_op jit(solution)/shard_map/ppermute | solution.py:23
  894.0 17.2 collective-permute-start.17
  900.2 12.6 collective-permute-start.22
  903.1 9.8 collective-permute-start.23
  969.7 996.7 %all-to-all-start.1 = ((f32[128,1,256]{2,1,0:T(1,128)}), f32[128,1,256]{2,1,0:T(1,128)S(1)}, u32[]{:S(2)}, u32[]{:S(2)}) async-start(f32[128,1,256]{2,1,0:T(1,128)} %reshape.107), calls=%async_computation.1 | async-start | bytes 262144 | tf_op jit(solution)/shard_map/all_to_all | solution.py:77
  975.5 936.8 %all-reduce.27.cloned.1.call-start = ((), (), s32[]{:S(2)}) async-start(), calls=%async_computation.2 | async-start | bytes 131072 | tf_op jit(solution)/shard_map/psum | solution.py:79
  976.4 988.7 %all-reduce.29.cloned.1.call-start = ((), (), s32[]{:S(2)}) async-start(), calls=%async_computation.3 | async-start | bytes 131072 | tf_op jit(solution)/shard_map/psum | solution.py:79
Sparse Core Ops, SparseCore 0:
  979.3 933.0 all-reduce.26
  1915.5 49.5 all-reduce.28
